TPU v7x, 512 devices: a whole 4x8x8 slice. The times are simulated.
512 devices in a mesh: ctx: 64 (over z, y), head: 8 (over x, core).
Axes of the slice: x: 4, y: 8, z: 8, core: 2. Of those that a mesh axis runs over, the one named last changes fastest.
Arguments:
- queries: bfloat16 [512, 8192], P('ctx', 'head'), may hold values from -6 to 6
- cache_keys: bfloat16 [65536, 8, 128], P('ctx', 'head'), may hold values from -6 to 6
- cache_values: bfloat16 [65536, 8, 128], P('ctx', 'head'), may hold values from -6 to 6
- vertical_blocks: int32 [64, 8], P('head'), may hold values from 0 to 511, as said below
- slash_offsets: int32 [64, 48], P('head'), may hold values from 0 to 511, as said below
- out_weight: bfloat16 [8192, 8192], P('head', 'ctx'), may hold values from -0.0625 to 0.0625
Outputs:
- projected: bfloat16 [512, 8192], P('head', 'ctx')
Inputs may be any that keep to these rules, and one draw needn't show every extreme that they name: `vertical_blocks`: every head's list holds block 0; entries may repeat, and a block counts once however often it is named. `slash_offsets`: every head's list holds offset 0; entries may repeat, and a block counts once however often it is reached.
All inputs are finite; a program needn't handle non-finite values.
Results may differ from a plain program's by a relative error of at most 0.007.
Values may be sent and summed in bfloat16 or wider, within the bound.
A program may use at most 64 MiB of HBM per device.

v0:
```python
from functools import partial
import jax
import jax.numpy as jnp
from jax import lax
from jax.sharding import PartitionSpec as P

BLOCK = 128
NEG_FILL = -1e30


def block_terms(q_four, key_block, value_block, allowed_mask, score_scale):
    kv_local = q_four.shape[1]
    group_size = q_four.shape[2]
    scores = (
        jnp.einsum("qgjd,kgd->qgjk", q_four, key_block, preferred_element_type=jnp.float32)
        * score_scale
    )
    scores = scores.reshape(scores.shape[0], kv_local * group_size, scores.shape[3])
    masked = jnp.where(allowed_mask, scores, NEG_FILL)
    block_peak = jnp.max(masked, axis=-1)
    safe_peak = jnp.where(block_peak > 0.5 * NEG_FILL, block_peak, 0.0)
    weights = jnp.where(allowed_mask, jnp.exp(scores - safe_peak[..., None]), 0.0).astype(
        jnp.bfloat16
    )
    block_total = jnp.sum(weights.astype(jnp.float32), axis=-1)
    weights_four = weights.reshape(weights.shape[0], kv_local, group_size, weights.shape[2])
    block_out = jnp.einsum(
        "qgjk,kgd->qgjd", weights_four, value_block, preferred_element_type=jnp.float32
    )
    return (
        block_peak,
        block_total,
        block_out.reshape(block_out.shape[0], kv_local * group_size, block_out.shape[3]),
    )


def body(queries, cache_keys, cache_values, vertical_blocks, slash_offsets, out_weight):
    ctx_count = lax.axis_size("ctx")
    ctx_place = lax.axis_index("ctx")
    q_whole = lax.all_gather(queries, "ctx", axis=0, tiled=True)
    q_total = q_whole.shape[0]
    local_len, kv_local, head_width = cache_keys.shape
    heads_local = vertical_blocks.shape[0]
    group_size = heads_local // kv_local
    local_blocks = local_len // BLOCK
    q_blocks = q_total // BLOCK
    all_blocks = local_blocks * ctx_count
    score_scale = float(head_width) ** (-0.5)
    q_four = q_whole.reshape(q_total, kv_local, group_size, head_width)
    block_ids = ctx_place * local_blocks + jnp.arange(local_blocks, dtype=jnp.int32)
    query_blocks = all_blocks - q_blocks + jnp.arange(q_blocks, dtype=jnp.int32)
    vertical_hit = jnp.any(vertical_blocks[:, :, None] == block_ids[None, None, :], axis=1)
    offsets = query_blocks[:, None] - block_ids[None, :]
    slash_hit = jnp.any(slash_offsets[:, None, None, :] == offsets[None, :, :, None], axis=3)
    chosen = jnp.transpose(vertical_hit[:, None, :] | slash_hit, (1, 0, 2))
    first_query = all_blocks * BLOCK - q_total
    query_pos = first_query + jnp.arange(q_total, dtype=jnp.int32)

    def visit_block(turn_index, state_carry, block_order):
        run_peak, run_total, run_out = state_carry
        local_block = block_order[turn_index]
        key_block = lax.dynamic_slice_in_dim(cache_keys, local_block * BLOCK, BLOCK, 0)
        value_block = lax.dynamic_slice_in_dim(cache_values, local_block * BLOCK, BLOCK, 0)
        picked = lax.dynamic_index_in_dim(chosen, local_block, 2, keepdims=False)
        picked_rows = jnp.repeat(picked, BLOCK, axis=0)
        key_pos = ctx_place * local_len + local_block * BLOCK + jnp.arange(BLOCK, dtype=jnp.int32)
        allowed_mask = picked_rows[:, :, None] & (
            key_pos[None, None, :] <= query_pos[:, None, None]
        )
        block_peak, block_total, block_out = block_terms(
            q_four, key_block, value_block, allowed_mask, score_scale
        )
        new_peak = jnp.maximum(run_peak, block_peak)
        old_factor = jnp.exp(run_peak - new_peak)
        new_factor = jnp.exp(block_peak - new_peak)
        new_total = run_total * old_factor + block_total * new_factor
        new_out = run_out * old_factor[..., None] + block_out * new_factor[..., None]
        return (new_peak, new_total, new_out)

    start_carry = (
        jnp.full((q_total, heads_local), NEG_FILL, jnp.float32),
        jnp.zeros((q_total, heads_local), jnp.float32),
        jnp.zeros((q_total, heads_local, head_width), jnp.float32),
    )
    block_order = jnp.arange(local_blocks, dtype=jnp.int32)
    local_peak, local_total, local_out = lax.fori_loop(
        0, local_blocks, partial(visit_block, block_order=block_order), start_carry
    )
    top_peak = lax.pmax(local_peak, "ctx")
    factor = jnp.exp(local_peak - top_peak)
    out_sum, total_sum = lax.psum((local_out * factor[..., None], local_total * factor), "ctx")
    attention = (
        (out_sum / total_sum[..., None])
        .reshape(q_total, heads_local * head_width)
        .astype(jnp.bfloat16)
    )
    return lax.psum_scatter(
        jnp.dot(attention, out_weight, preferred_element_type=jnp.float32),
        "head",
        scatter_dimension=0,
        tiled=True,
    ).astype(jnp.bfloat16)


def solution(mesh):
    return jax.shard_map(
        body,
        mesh=mesh,
        in_specs=(
            P("ctx", "head"),
            P("ctx", "head", None),
            P("ctx", "head", None),
            P("head", None),
            P("head", None),
            P("head", "ctx"),
        ),
        out_specs=P("head", "ctx"),
        check_vma=False,
    )
```

profile of v0, /device:TPU:8, one launch (start us, length us, event | category | flops | bytes accessed | tf_op | source)
XLA Modules:
  0.0 755.4 jit_solution(7034202437298603779)
XLA Ops:
  6.5 0.7 all-gather.2.cloned.1.call-update
  7.4 0.8 compare_reduce_fusion.1
  8.2 1.4 compare_reduce_fusion
  9.7 86.6 %all-gather.2.cloned.1.call-done = bf16[512,1024]{1,0:T(8,128)(2,1)} async-done(((bf16[8,1024]{1,0:T(8,128)(2,1)}), bf16[512,1024]{1,0:T(8,128)(2,1)}) %all-gather.2.cloned.1.call-update) | async-done | bytes 1048592 | tf_op jit(solution)/shard_map/all_gather | solution.py:40
  96.3 2.3 copy.18
  98.6 1.6 copy.20
  100.3 60.9 %while.20 = (s32[]{:T(128)}, f32[512,8]{0,1:T(8,128)S(1)}, f32[512,8]{0,1:T(8,128)S(1)}, f32[512,8,128]{0,2,1:T(8,128)S(1)}, s32[8]{0:T(128)S(1)}, /*index=5*/pr...) while((s32[]{:T(128)}, f32[512,8]{0,1:T(8,128)S(1)}, ...), condition=%wide.region_5.6_spmd.clone, body=%wide.region_2.5_spmd.clone.sunk | while | flops 279020160 | bytes 12146040 | solution.py:86
  100.3 0.7 dynamic_slice.59
  103.9 1.3 fusion.38
  105.9 1.9 fusion.40
  107.9 0.7 dynamic_slice.59
  111.5 1.3 fusion.38
  113.5 1.9 fusion.40
  119.2 1.3 fusion.38
  121.1 1.9 fusion.40
  126.8 1.3 fusion.38
  128.8 1.9 fusion.40
  134.4 1.3 fusion.38
  136.4 1.9 fusion.40
  142.0 1.3 fusion.38
  144.0 1.9 fusion.40
  149.6 1.3 fusion.38
  151.6 1.9 fusion.40
  157.2 1.3 fusion.38
  159.2 1.9 fusion.40
  161.2 272.2 %pmax.7 = f32[512,8]{0,1:T(8,128)S(1)} all-reduce(f32[512,8]{0,1:T(8,128)S(1)} %get-tuple-element.262), channel_id=1, replica_groups=mesh['ctx'=64,'head'=8] {'ctx'}, use_global_device_ids=true, to_apply=%region_6.7 | all-reduce | flops 4096 | bytes 32768 | tf_op jit(solution)/shard_map/pmax | solution.py:89
  433.4 1.6 broadcast_multiply_fusion
  435.1 276.5 %psum.15 = f32[512,8]{0,1:T(8,128)S(1)} all-reduce(f32[512,8]{0,1:T(8,128)S(1)} %get-tuple-element.363), channel_id=1, replica_groups=mesh['ctx'=64,'head'=8] {'ctx'}, use_global_device_ids=true, to_apply=%region_8.9 | all-reduce | flops 4096 | bytes 32768 | tf_op jit(solution)/shard_map/psum | solution.py:91
  711.6 1.9 divide_convert_fusion
  713.5 1.2 fusion.28
  714.7 32.8 %reduce-scatter.2.cloned.1.call-done = f32[64,128]{1,0:T(8,128)} async-done(((f32[512,128]{1,0:T(8,128)}), f32[64,128]{1,0:T(8,128)}) %reduce-scatter.2.cloned.1.call-update) | async-done | bytes 32784 | tf_op jit(solution)/shard_map/reduce_scatter | solution.py:97
  747.5 1.4 convert_element_type.36
  (88 shorter events, 10.8 us)
Async XLA Ops:
  6.5 706.9 %copy-start = (bf16[1024,128]{1,0:T(8,128)(2,1)S(1)}, bf16[1024,128]{1,0:T(8,128)(2,1)}, u32[]{:S(2)}) copy-start(bf16[1024,128]{1,0:T(8,128)(2,1)} %param.13) | copy-start | bytes 786436
  6.5 89.8 %all-gather.2.cloned.1.call-start = ((), (), s32[]{:S(2)}) async-start(), calls=%async_computation.1 | async-start | bytes 1064960 | tf_op jit(solution)/shard_map/all_gather | solution.py:40
  7.3 704.3 %all-reduce.2.cloned.1.call-start = ((), (), s32[]{:S(2)}) async-start(), calls=%async_computation.2 | async-start | bytes 4194304 | tf_op jit(solution)/shard_map/psum | solution.py:91
  435.1 312.4 %reduce-scatter.2.cloned.1.call-start = ((), (), s32[]{:S(2)}) async-start(), calls=%async_computation.3 | async-start | bytes 294912 | tf_op jit(solution)/shard_map/reduce_scatter | solution.py:97
Sparse Core Ops, SparseCore 0:
  10.4 85.8 all-gather.1
  435.2 162.4 all-reduce.1
  714.8 32.6 reduce-scatter.1
where the time goes:
time: 757 us; the launch traced here: 755 us
  blocking collectives  549 us (73%)
  waiting for transfers between devices  120 us (16%)
  matrix products  27.4 us (4%)
  loops' own time  22.9 us (3%)
  between operations  13.2 us (2%)
  other arithmetic  12.9 us (2%)
  local copies, waits for them, and re-layouts  10 us (1%)
    psum x1, blocking collectives, body(): lax.psum((local_out * factor[..., None], local_total * factor), 'ctx')  276 us
    pmax x1, blocking collectives, body(): top_peak = lax.pmax(local_peak, 'ctx')  272 us
    all_gather x1, waiting for transfers between devices, body(): q_whole = lax.all_gather(queries, 'ctx', axis=0, tiled=True)  86.6 us
    reduce_scatter x1, waiting for transfers between devices, body(): lax.psum_scatter(jnp.dot(attention, out_weight, preferred_element_type=jn...  32.8 us
    another operation x1, loops' own time, body(): lax.fori_loop(0, local_blocks, partial(visit_block, block_order=block_ord...  22.9 us
    dot_general x8, matrix products, block_terms(): jnp.einsum('qgjk,kgd->qgjd', weights_four, value_block, preferred_element...  15.5 us
  transfers between devices with their start and end apart: 3, of which 2 were waited for; matrix products, arithmetic and copies ran while one was open for 0% of the time, Pallas kernels for 0%

commit v1 on v0

--- a/solution.py
+++ b/solution.py
@@ -37,7 +37,9 @@
 def body(queries, cache_keys, cache_values, vertical_blocks, slash_offsets, out_weight):
     ctx_count = lax.axis_size("ctx")
     ctx_place = lax.axis_index("ctx")
-    q_whole = lax.all_gather(queries, "ctx", axis=0, tiled=True)
+    q_whole = jnp.concatenate(
+        lax.all_to_all(jnp.stack([queries] * lax.axis_size("ctx")), "ctx", 0, 0), axis=0
+    )
     q_total = q_whole.shape[0]
     local_len, kv_local, head_width = cache_keys.shape
     heads_local = vertical_blocks.shape[0]

time: 757 us -> 710 us (0.938)
  waiting for transfers between devices: 120 us -> 59.6 us
  starting transfers between devices: 0.08 us -> 16.7 us
    all_gather x1 -> x0, waiting for transfers between devices: 86.6 us -> none  [body(): q_whole = lax.all_gather(queries, 'ctx', axis=0, tiled=True)]
    all_to_all x0 -> x1, waiting for transfers between devices: none -> 28.1 us  [body(): lax.all_to_all(jnp.stack([queries] * lax.axis_size('ctx')), 'ctx', 0, 0)]
    all_to_all x0 -> x1, starting transfers between devices: none -> 16.6 us  [body(): lax.all_to_all(jnp.stack([queries] * lax.axis_size('ctx')), 'ctx', 0, 0)]
where the time goes in v1:
time: 710 us; the launch traced here: 709 us
  blocking collectives  549 us (77%)
  waiting for transfers between devices  59.6 us (8%)
  matrix products  27.4 us (4%)
  loops' own time  22.9 us (3%)
  starting transfers between devices  16.7 us (2%)
  between operations  13.5 us (2%)
  other arithmetic  11.6 us (2%)
  local copies, waits for them, and re-layouts  8.39 us (1%)
    psum x1, blocking collectives, body(): lax.psum((local_out * factor[..., None], local_total * factor), 'ctx')  277 us
    pmax x1, blocking collectives, body(): top_peak = lax.pmax(local_peak, 'ctx')  272 us
    reduce_scatter x1, waiting for transfers between devices, body(): lax.psum_scatter(jnp.dot(attention, out_weight, preferred_element_type=jn...  31.4 us
    all_to_all x1, waiting for transfers between devices, body(): lax.all_to_all(jnp.stack([queries] * lax.axis_size('ctx')), 'ctx', 0, 0)  28.1 us
    another operation x1, loops' own time, body(): lax.fori_loop(0, local_blocks, partial(visit_block, block_order=block_ord...  22.9 us
    all_to_all x1, starting transfers between devices, body(): lax.all_to_all(jnp.stack([queries] * lax.axis_size('ctx')), 'ctx', 0, 0)  16.6 us
    dot_general x8, matrix products, block_terms(): jnp.einsum('qgjk,kgd->qgjd', weights_four, value_block, preferred_element...  15.5 us
  transfers between devices with their start and end apart: 3, of which 2 were waited for; matrix products, arithmetic and copies ran while one was open for 0% of the time, Pallas kernels for 0%

profile of v1, /device:TPU:8, one launch (start us, length us, event | category | flops | bytes accessed | tf_op | source)
XLA Modules:
  0.0 708.8 jit_solution(7103123090716757143)
XLA Ops:
  6.5 1.9 stack.2
  8.4 16.6 %all-to-all-start = ((bf16[64,8,1024]{2,1,0:T(8,128)(2,1)}), bf16[64,8,1024]{2,1,0:T(8,128)(2,1)S(1)}, u32[]{:S(2)}, u32[]{:S(2)}) async-start(bf16[64,8,1024]{2,1,0:T(8,128)(2,1)} %stack.2), calls=%async_computation | async-start | bytes 2097152 | tf_op jit(solution)/shard_map/all_to_all | solution.py:41
  25.3 0.7 compare_reduce_fusion
  26.1 28.1 %all-to-all-done = bf16[64,8,1024]{2,1,0:T(8,128)(2,1)S(1)} async-done(((bf16[64,8,1024]{2,1,0:T(8,128)(2,1)}), bf16[64,8,1024]{2,1,0:T(8,128)(2,1)S(1)}, u32[]{:S(2)}, u32[]{:S(2)}) %all-to-all-start) | async-done | bytes 1048608 | tf_op jit(solution)/shard_map/all_to_all | solution.py:41
  54.7 60.9 %while.20 = (s32[]{:T(128)}, f32[512,8]{0,1:T(8,128)S(1)}, f32[512,8]{0,1:T(8,128)S(1)}, f32[512,8,128]{0,2,1:T(8,128)S(1)}, s32[8]{0:T(128)S(1)}, /*index=5*/pr...) while((s32[]{:T(128)}, f32[512,8]{0,1:T(8,128)S(1)}, ...), condition=%wide.region_5.6_spmd.clone, body=%wide.region_2.5_spmd.clone.sunk | while | flops 279020160 | bytes 12146040 | solution.py:88
  54.7 0.7 dynamic_slice.59
  58.4 1.3 fusion.38
  60.4 1.9 fusion.40
  62.3 0.7 dynamic_slice.59
  66.0 1.3 fusion.38
  68.0 1.9 fusion.40
  73.6 1.3 fusion.38
  75.6 1.9 fusion.40
  77.5 0.7 dynamic_slice.59
  81.2 1.3 fusion.38
  83.2 1.9 fusion.40
  85.2 0.7 dynamic_slice.59
  88.8 1.3 fusion.38
  90.8 1.9 fusion.40
  96.4 1.3 fusion.38
  98.4 1.9 fusion.40
  104.0 1.3 fusion.38
  106.0 1.9 fusion.40
  111.7 1.3 fusion.38
  113.6 1.9 fusion.40
  115.6 271.9 %pmax.7 = f32[512,8]{0,1:T(8,128)S(1)} all-reduce(f32[512,8]{0,1:T(8,128)S(1)} %get-tuple-element.262), channel_id=1, replica_groups=mesh['ctx'=64,'head'=8] {'ctx'}, use_global_device_ids=true, to_apply=%region_6.7 | all-reduce | flops 4096 | bytes 32768 | tf_op jit(solution)/shard_map/pmax | solution.py:91
  387.5 1.6 broadcast_multiply_fusion
  389.2 276.8 %psum.15 = f32[512,8]{0,1:T(8,128)S(1)} all-reduce(f32[512,8]{0,1:T(8,128)S(1)} %get-tuple-element.353), channel_id=1, replica_groups=mesh['ctx'=64,'head'=8] {'ctx'}, use_global_device_ids=true, to_apply=%region_8.9 | all-reduce | flops 4096 | bytes 32768 | tf_op jit(solution)/shard_map/psum | solution.py:93
  666.1 1.9 divide_convert_fusion
  667.9 1.2 fusion.28
  669.1 31.4 %reduce-scatter.2.cloned.1.call-done = f32[64,128]{1,0:T(8,128)} async-done(((f32[512,128]{1,0:T(8,128)}), f32[64,128]{1,0:T(8,128)}) %reduce-scatter.2.cloned.1.call-update) | async-done | bytes 32784 | tf_op jit(solution)/shard_map/reduce_scatter | solution.py:99
  700.6 1.4 convert_element_type.36
  (92 shorter events, 10.0 us)
Async XLA Ops:
  6.5 661.4 %copy-start = (bf16[1024,128]{1,0:T(8,128)(2,1)S(1)}, bf16[1024,128]{1,0:T(8,128)(2,1)}, u32[]{:S(2)}) copy-start(bf16[1024,128]{1,0:T(8,128)(2,1)} %param.13) | copy-start | bytes 786436
  6.5 18.6 %copy-start.1 = (s32[8,8]{1,0:T(8,128)S(1)}, s32[8,8]{1,0:T(8,128)}, u32[]{:S(2)}) copy-start(s32[8,8]{1,0:T(8,128)} %param.11) | copy-start | bytes 772
  6.5 18.8 %copy-start.2 = (s32[8,48]{1,0:T(8,128)S(1)}, s32[8,48]{1,0:T(8,128)}, u32[]{:S(2)}) copy-start(s32[8,48]{1,0:T(8,128)} %param.12) | copy-start | bytes 4612
  8.4 45.8 %all-to-all-start = ((bf16[64,8,1024]{2,1,0:T(8,128)(2,1)}), bf16[64,8,1024]{2,1,0:T(8,128)(2,1)S(1)}, u32[]{:S(2)}, u32[]{:S(2)}) async-start(bf16[64,8,1024]{2,1,0:T(8,128)(2,1)} %stack.2), calls=%async_computation | async-start | bytes 2097152 | tf_op jit(solution)/shard_map/all_to_all | solution.py:41
  25.0 641.0 %all-reduce.2.cloned.1.call-start = ((), (), s32[]{:S(2)}) async-start(), calls=%async_computation.2 | async-start | bytes 4194304 | tf_op jit(solution)/shard_map/psum | solution.py:93
  389.2 311.4 %reduce-scatter.2.cloned.1.call-start = ((), (), s32[]{:S(2)}) async-start(), calls=%async_computation.3 | async-start | bytes 294912 | tf_op jit(solution)/shard_map/reduce_scatter | solution.py:99
Sparse Core Ops, SparseCore 0:
  389.3 160.9 all-reduce.1
  669.3 31.2 reduce-scatter.1
